TPU v7x, 256 devices: a whole 4x4x8 slice. The times are simulated.
256 devices in a mesh: gx: 8 (over x, core), gyz: 8 (over y, z_lo), band: 4 (over z_hi).
Axes of the slice: x: 4, y: 4, z: 8 (z_hi: 4, z_lo: 2; z = z_hi * 2 + z_lo), core: 2. Of those that a mesh axis runs over, the one named last changes fastest.
Arguments:
- orbitals: float32 [256, 32, 64, 128], P('band', 'gx', 'gyz'), may hold values from -6 to 6
- v_local: float32 [32, 64, 128], P('gx', 'gyz'), may hold values from 0 to 2
- features: bfloat16 [11, 32, 64, 128], P(None, 'gx', 'gyz'), may hold values from -6 to 6
- w_first: bfloat16 [256, 11], replicated, may hold values from -1.75 to 1.75
- w_hidden: bfloat16 [1, 256, 256], replicated, may hold values from -0.375 to 0.375
- w_last: bfloat16 [256], replicated, may hold values from -0.375 to 0.375
- rotation: float32 [256, 256], replicated, may hold values from -0.375 to 0.375
- assignment: int32 [256], replicated, may hold values from 0 to 255, each once
- degrees: int32 [256], P('band'), may hold values from 4 to 8, as said below
Outputs:
- gram: float32 [256, 256], P('band')
- rotated: float32 [256, 32, 64, 128], P('band', 'gx', 'gyz')
Inputs may be any that keep to these rules, and one draw needn't show every extreme that they name: `degrees`: a filter degree of each slot; some slot has 8 and some has 4. `assignment`: each orbital is held in exactly one slot.
All inputs are finite; a program needn't handle non-finite values.
Results may differ from a plain program's by a relative error of at most 0.0043.
Values may be sent and summed in bfloat16 or wider, within the bound.
No kernel may reach another device: no remote copies, remote signals or barrier semaphores. Data moves between devices by JAX's collectives and lax.ppermute only.
A program may use at most 64 MiB of HBM per device.

v0:
```python
import jax
import jax.numpy as jnp
from jax import lax
from jax.sharding import PartitionSpec as P

DEG = 8
LOWER_EDGE = 2.0
CUT_EDGE = 3.0
UPPER_EDGE = 9.5


def with_halo(block, sides, width):
    for axis, dim in sides:
        count = lax.axis_size(axis)
        forward = [(i, i + 1) for i in range(count - 1)]
        backward = [(target, source) for source, target in forward]
        low = lax.ppermute(
            lax.slice_in_dim(block, block.shape[dim] - width, None, axis=dim), axis, forward
        )
        high = lax.ppermute(lax.slice_in_dim(block, 0, width, axis=dim), axis, backward)
        block = jnp.concatenate([low, block, high], axis=dim)
    return block


def coefficients(count):
    half_width = (UPPER_EDGE - CUT_EDGE) / 2.0
    centre = (UPPER_EDGE + CUT_EDGE) / 2.0
    first = half_width / (LOWER_EDGE - centre)
    factors = [(first / half_width, 0.0)]
    sigma = first
    for rounds in range(1, count):
        updated = 1.0 / (2.0 / first - sigma)
        factors.append((2.0 * updated / half_width, sigma * updated))
        sigma = updated
    return (factors, centre)


def hamiltonian(field, potential):
    padded = with_halo(field, (("gx", 1), ("gyz", 2)), 1)
    padded = jnp.pad(padded, ((0, 0), (0, 0), (0, 0), (1, 1)))
    beside_all = padded[:, 2:, 1:-1, 1:-1] + padded[:, :-2, 1:-1, 1:-1]
    beside_all = beside_all + padded[:, 1:-1, 2:, 1:-1] + padded[:, 1:-1, :-2, 1:-1]
    beside_all = beside_all + padded[:, 1:-1, 1:-1, 2:] + padded[:, 1:-1, 1:-1, :-2]
    return 0.5 * (6.0 * field - beside_all) + potential * field


def network(cell_features, w_first, w_hidden, w_last):
    feature_count = cell_features.shape[0]
    flattened = cell_features.reshape(feature_count, -1)
    hidden = jax.nn.silu(jnp.dot(w_first, flattened, preferred_element_type=jnp.float32)).astype(
        jnp.bfloat16
    )
    hidden = jax.nn.silu(jnp.dot(w_hidden[0], hidden, preferred_element_type=jnp.float32)).astype(
        jnp.bfloat16
    )
    values = jnp.tanh(jnp.dot(w_last[None, :], hidden, preferred_element_type=jnp.float32)[0])
    return values.reshape(cell_features.shape[1:])


def on_device(
    orbitals, v_local, features, w_first, w_hidden, w_last, rotation, assignment, degrees
):
    group = lax.axis_index("band")
    local_slots, size_x, size_y, size_z = orbitals.shape
    total_slots = rotation.shape[0]
    cells = size_x * size_y * size_z
    total_cells = float(cells * lax.axis_size("gx") * lax.axis_size("gyz"))
    xc_field = network(features, w_first, w_hidden, w_last)
    potential = v_local + xc_field
    factors, centre = coefficients(DEG)
    previous = orbitals
    current = orbitals
    for rounds in range(DEG):
        image = hamiltonian(current, potential)
        scale_new, scale_old = factors[rounds]
        updated = scale_new * (image - centre * current) - scale_old * previous
        active = (degrees > rounds)[:, None, None, None]
        previous = jnp.where(active, current, previous)
        current = jnp.where(active, updated, current)
    filtered = current.astype(jnp.bfloat16).reshape(local_slots, cells)
    select = (assignment[:, None] == lax.iota(jnp.int32, total_slots)[None, :]).astype(jnp.float32)
    permuted = jnp.dot(select, rotation, precision=lax.Precision.HIGHEST)
    slot_rotation = jnp.dot(permuted, select.T, precision=lax.Precision.HIGHEST).astype(
        jnp.bfloat16
    )
    own_columns = lax.dynamic_slice_in_dim(slot_rotation, group * local_slots, local_slots, 1)
    shard_rows = lax.all_gather(filtered, "band", axis=0, tiled=True)
    margin = lax.dot_general(
        filtered, shard_rows, (((1,), (1,)), ((), ())), preferred_element_type=jnp.float32
    )
    gram_part = margin
    rotated_part = lax.dot_general(
        own_columns, shard_rows, (((0,), (0,)), ((), ())), preferred_element_type=jnp.float32
    )
    gram_part, rotated_flat = (gram_part, rotated_part)
    gram = lax.psum(gram_part, ("gx", "gyz")) / total_cells
    rotated = rotated_flat.reshape(local_slots, size_x, size_y, size_z)
    return (gram, rotated)


def solution(mesh):
    placed = (
        P("band", "gx", "gyz", None),
        P("gx", "gyz", None),
        P(None, "gx", "gyz", None),
        P(),
        P(),
        P(),
        P(),
        P(),
        P("band"),
    )
    return jax.shard_map(
        on_device,
        mesh=mesh,
        in_specs=placed,
        out_specs=(P("band", None), P("band", "gx", "gyz", None)),
        check_vma=False,
    )
```

profile of v0, /device:TPU:8, one launch (start us, length us, event | category | flops | bytes accessed | tf_op | source)
XLA Modules:
  0.0 750.5 jit_solution(973591448265603997)
XLA Ops:
  13.8 3.4 multiply_convert_fusion.1
  17.3 3.3 fusion.1
  21.3 3.7 collective-permute-start.2
  25.1 2.1 collective-permute-start.3
  29.3 6.6 collective-permute-done.3
  39.2 3.0 collective-permute-start.5
  45.5 3.8 collective-permute-start.7
  51.0 3.5 collective-permute-done.7
  59.2 4.8 collective-permute-start.9
  67.1 3.9 collective-permute-start.11
  72.7 4.7 collective-permute-done.11
  77.4 2.1 select_maximum_fusion.20
  82.6 5.3 collective-permute-start.13
  91.0 4.1 collective-permute-start.15
  96.6 4.7 collective-permute-done.15
  101.3 2.1 select_maximum_fusion.16
  106.7 5.3 collective-permute-start.17
  115.0 3.9 collective-permute-start.19
  120.7 4.7 collective-permute-done.19
  125.4 2.1 select_maximum_fusion.12
  130.1 5.3 collective-permute-start.21
  138.5 3.9 collective-permute-start.23
  144.2 4.7 collective-permute-done.23
  154.0 5.3 collective-permute-start.25
  162.3 3.9 collective-permute-start.27
  168.0 4.7 collective-permute-done.27
  177.4 5.3 collective-permute-start.29
  185.8 3.9 collective-permute-start.31
  191.4 4.7 collective-permute-done.31
  201.8 60.9 %all-gather.2.cloned.1.call-done = bf16[256,4096]{1,0:T(8,128)(2,1)} async-done(((bf16[64,4096]{1,0:T(8,128)(2,1)}), bf16[256,4096]{1,0:T(8,128)(2,1)}) %all-gather.2.cloned.1.call-update) | async-done | bytes 2097168 | tf_op jit(solution)/shard_map/all_gather | solution.py:87
  262.7 3.2 fusion.91
  267.6 474.6 %all-reduce.10.cloned.1.call-done = f32[64,256]{1,0:T(8,128)} async-done(((f32[64,256]{1,0:T(8,128)}), f32[64,256]{1,0:T(8,128)}) %all-reduce.10.cloned.1.call-update) | async-done | bytes 65552 | tf_op jit(solution)/shard_map/psum | solution.py:96
  (101 shorter events, 77.9 us)
Async XLA Ops:
  7.2 255.5 %all-gather.2.cloned.1.call-start = ((), (), s32[]{:S(2)}) async-start(), calls=%async_computation | async-start | bytes 2621440 | tf_op jit(solution)/shard_map/all_gather | solution.py:87
  9.1 11.5 %collective-permute-start.1 = (f32[64,1,8,128]{3,0,2,1:T(8,128)S(1)}, f32[64,1,8,128]{3,0,2,1:T(8,128)S(1)}, u32[]{:S(2)}, u32[]{:S(2)}) collective-permute-start(f32[64,1,8,128]{3,0,2,1:T(8,128)S(1)} %get-tuple-element.37), channel_id=1, source_target_pairs={{0,32},{32,64},{64,96},{96,128},{128,160},{160,192},{192,224},{1,3... | collective-permute-start | bytes 786440 | tf_op jit(solution)/shard_map/ppermute | solution.py:17
  10.9 10.4 %collective-permute-start = (f32[64,1,8,128]{3,0,2,1:T(8,128)S(1)}, f32[64,1,8,128]{3,0,2,1:T(8,128)S(1)}, u32[]{:S(2)}, u32[]{:S(2)}) collective-permute-start(f32[64,1,8,128]{3,0,2,1:T(8,128)S(1)} %get-tuple-element.36), channel_id=1, source_target_pairs={{32,0},{64,32},{96,64},{128,96},{160,128},{192,160},{224,192},{33,... | collective-permute-start | bytes 786440 | tf_op jit(solution)/shard_map/ppermute | solution.py:20
  21.3 8.0 %collective-permute-start.2 = (f32[64,6,1,128]{3,0,2,1:T(8,128)S(1)}, f32[64,6,1,128]{3,0,2,1:T(8,128)S(1)}, u32[]{:S(2)}, u32[]{:S(2)}) collective-permute-start(f32[64,6,1,128]{3,0,2,1:T(8,128)S(1)} %get-tuple-element.21), channel_id=1, source_target_pairs={{4,0},{8,4},{12,8},{16,12},{20,16},{24,20},{28,24},{5,1},{9,5},{13... | collective-permute-start | bytes 589832 | tf_op jit(solution)/shard_map/ppermute | solution.py:20
  25.1 10.9 %collective-permute-start.3 = (f32[64,6,1,128]{3,0,2,1:T(8,128)S(1)}, f32[64,6,1,128]{3,0,2,1:T(8,128)S(1)}, u32[]{:S(2)}, u32[]{:S(2)}) collective-permute-start(f32[64,6,1,128]{3,0,2,1:T(8,128)S(1)} %get-tuple-element.20), channel_id=1, source_target_pairs={{0,4},{4,8},{8,12},{12,16},{16,20},{20,24},{24,28},{1,5},{5,9},{9,... | collective-permute-start | bytes 589832 | tf_op jit(solution)/shard_map/ppermute | solution.py:17
  43.4 7.6 %collective-permute-start.6 = (f32[64,6,1,128]{3,0,2,1:T(8,128)S(1)}, f32[64,6,1,128]{3,0,2,1:T(8,128)S(1)}, u32[]{:S(2)}, u32[]{:S(2)}) collective-permute-start(f32[64,6,1,128]{3,0,2,1:T(8,128)S(1)} %get-tuple-element.19), channel_id=1, source_target_pairs={{4,0},{8,4},{12,8},{16,12},{20,16},{24,20},{28,24},{5,1},{9,5},{13... | collective-permute-start | bytes 589832 | tf_op jit(solution)/shard_map/ppermute | solution.py:20
  45.5 9.0 %collective-permute-start.7 = (f32[64,6,1,128]{3,0,2,1:T(8,128)S(1)}, f32[64,6,1,128]{3,0,2,1:T(8,128)S(1)}, u32[]{:S(2)}, u32[]{:S(2)}) collective-permute-start(f32[64,6,1,128]{3,0,2,1:T(8,128)S(1)} %get-tuple-element.18), channel_id=1, source_target_pairs={{0,4},{4,8},{8,12},{12,16},{16,20},{20,24},{24,28},{1,5},{5,9},{9,... | collective-permute-start | bytes 589832 | tf_op jit(solution)/shard_map/ppermute | solution.py:17
  57.9 6.1 collective-permute-start.8
  59.2 5.9 collective-permute-start.9
  65.1 7.6 %collective-permute-start.10 = (f32[64,6,1,128]{3,0,2,1:T(8,128)S(1)}, f32[64,6,1,128]{3,0,2,1:T(8,128)S(1)}, u32[]{:S(2)}, u32[]{:S(2)}) collective-permute-start(f32[64,6,1,128]{3,0,2,1:T(8,128)S(1)} %get-tuple-element.17), channel_id=1, source_target_pairs={{4,0},{8,4},{12,8},{16,12},{20,16},{24,20},{28,24},{5,1},{9,5},{13... | collective-permute-start | bytes 589832 | tf_op jit(solution)/shard_map/ppermute | solution.py:20
  67.1 10.4 %collective-permute-start.11 = (f32[64,6,1,128]{3,0,2,1:T(8,128)S(1)}, f32[64,6,1,128]{3,0,2,1:T(8,128)S(1)}, u32[]{:S(2)}, u32[]{:S(2)}) collective-permute-start(f32[64,6,1,128]{3,0,2,1:T(8,128)S(1)} %get-tuple-element.16), channel_id=1, source_target_pairs={{0,4},{4,8},{8,12},{12,16},{16,20},{20,24},{24,28},{1,5},{5,9},{9,... | collective-permute-start | bytes 589832 | tf_op jit(solution)/shard_map/ppermute | solution.py:17
  81.3 6.6 collective-permute-start.12
  82.6 6.4 collective-permute-start.13
  89.0 7.6 %collective-permute-start.14 = (f32[64,6,1,128]{3,0,2,1:T(8,128)S(1)}, f32[64,6,1,128]{3,0,2,1:T(8,128)S(1)}, u32[]{:S(2)}, u32[]{:S(2)}) collective-permute-start(f32[64,6,1,128]{3,0,2,1:T(8,128)S(1)} %get-tuple-element.15), channel_id=1, source_target_pairs={{4,0},{8,4},{12,8},{16,12},{20,16},{24,20},{28,24},{5,1},{9,5},{13... | collective-permute-start | bytes 589832 | tf_op jit(solution)/shard_map/ppermute | solution.py:20
  91.0 10.4 %collective-permute-start.15 = (f32[64,6,1,128]{3,0,2,1:T(8,128)S(1)}, f32[64,6,1,128]{3,0,2,1:T(8,128)S(1)}, u32[]{:S(2)}, u32[]{:S(2)}) collective-permute-start(f32[64,6,1,128]{3,0,2,1:T(8,128)S(1)} %get-tuple-element.14), channel_id=1, source_target_pairs={{0,4},{4,8},{8,12},{12,16},{16,20},{20,24},{24,28},{1,5},{5,9},{9,... | collective-permute-start | bytes 589832 | tf_op jit(solution)/shard_map/ppermute | solution.py:17
  105.4 6.6 collective-permute-start.16
  106.7 6.4 collective-permute-start.17
  113.1 7.6 %collective-permute-start.18 = (f32[64,6,1,128]{3,0,2,1:T(8,128)S(1)}, f32[64,6,1,128]{3,0,2,1:T(8,128)S(1)}, u32[]{:S(2)}, u32[]{:S(2)}) collective-permute-start(f32[64,6,1,128]{3,0,2,1:T(8,128)S(1)} %get-tuple-element.13), channel_id=1, source_target_pairs={{4,0},{8,4},{12,8},{16,12},{20,16},{24,20},{28,24},{5,1},{9,5},{13... | collective-permute-start | bytes 589832 | tf_op jit(solution)/shard_map/ppermute | solution.py:20
  115.0 10.4 %collective-permute-start.19 = (f32[64,6,1,128]{3,0,2,1:T(8,128)S(1)}, f32[64,6,1,128]{3,0,2,1:T(8,128)S(1)}, u32[]{:S(2)}, u32[]{:S(2)}) collective-permute-start(f32[64,6,1,128]{3,0,2,1:T(8,128)S(1)} %get-tuple-element.12), channel_id=1, source_target_pairs={{0,4},{4,8},{8,12},{12,16},{16,20},{20,24},{24,28},{1,5},{5,9},{9,... | collective-permute-start | bytes 589832 | tf_op jit(solution)/shard_map/ppermute | solution.py:17
  128.8 6.6 collective-permute-start.20
  130.1 6.4 collective-permute-start.21
  136.6 7.6 %collective-permute-start.22 = (f32[64,6,1,128]{3,0,2,1:T(8,128)S(1)}, f32[64,6,1,128]{3,0,2,1:T(8,128)S(1)}, u32[]{:S(2)}, u32[]{:S(2)}) collective-permute-start(f32[64,6,1,128]{3,0,2,1:T(8,128)S(1)} %get-tuple-element.11), channel_id=1, source_target_pairs={{4,0},{8,4},{12,8},{16,12},{20,16},{24,20},{28,24},{5,1},{9,5},{13... | collective-permute-start | bytes 589832 | tf_op jit(solution)/shard_map/ppermute | solution.py:20
  138.5 10.4 %collective-permute-start.23 = (f32[64,6,1,128]{3,0,2,1:T(8,128)S(1)}, f32[64,6,1,128]{3,0,2,1:T(8,128)S(1)}, u32[]{:S(2)}, u32[]{:S(2)}) collective-permute-start(f32[64,6,1,128]{3,0,2,1:T(8,128)S(1)} %get-tuple-element.10), channel_id=1, source_target_pairs={{0,4},{4,8},{8,12},{12,16},{16,20},{20,24},{24,28},{1,5},{5,9},{9,... | collective-permute-start | bytes 589832 | tf_op jit(solution)/shard_map/ppermute | solution.py:17
  152.7 6.6 collective-permute-start.24
  154.0 6.4 collective-permute-start.25
  160.4 7.6 %collective-permute-start.26 = (f32[64,6,1,128]{3,0,2,1:T(8,128)S(1)}, f32[64,6,1,128]{3,0,2,1:T(8,128)S(1)}, u32[]{:S(2)}, u32[]{:S(2)}) collective-permute-start(f32[64,6,1,128]{3,0,2,1:T(8,128)S(1)} %get-tuple-element.9), channel_id=1, source_target_pairs={{4,0},{8,4},{12,8},{16,12},{20,16},{24,20},{28,24},{5,1},{9,5},{13... | collective-permute-start | bytes 589832 | tf_op jit(solution)/shard_map/ppermute | solution.py:20
  162.3 10.4 %collective-permute-start.27 = (f32[64,6,1,128]{3,0,2,1:T(8,128)S(1)}, f32[64,6,1,128]{3,0,2,1:T(8,128)S(1)}, u32[]{:S(2)}, u32[]{:S(2)}) collective-permute-start(f32[64,6,1,128]{3,0,2,1:T(8,128)S(1)} %get-tuple-element.8), channel_id=1, source_target_pairs={{0,4},{4,8},{8,12},{12,16},{16,20},{20,24},{24,28},{1,5},{5,9},{9,... | collective-permute-start | bytes 589832 | tf_op jit(solution)/shard_map/ppermute | solution.py:17
  176.1 6.6 collective-permute-start.28
  177.4 6.4 collective-permute-start.29
  183.9 7.6 %collective-permute-start.30 = (f32[64,6,1,128]{3,0,2,1:T(8,128)S(1)}, f32[64,6,1,128]{3,0,2,1:T(8,128)S(1)}, u32[]{:S(2)}, u32[]{:S(2)}) collective-permute-start(f32[64,6,1,128]{3,0,2,1:T(8,128)S(1)} %get-tuple-element.7), channel_id=1, source_target_pairs={{4,0},{8,4},{12,8},{16,12},{20,16},{24,20},{28,24},{5,1},{9,5},{13... | collective-permute-start | bytes 589832 | tf_op jit(solution)/shard_map/ppermute | solution.py:20
  185.8 10.4 %collective-permute-start.31 = (f32[64,6,1,128]{3,0,2,1:T(8,128)S(1)}, f32[64,6,1,128]{3,0,2,1:T(8,128)S(1)}, u32[]{:S(2)}, u32[]{:S(2)}) collective-permute-start(f32[64,6,1,128]{3,0,2,1:T(8,128)S(1)} %get-tuple-element.6), channel_id=1, source_target_pairs={{0,4},{4,8},{8,12},{12,16},{16,20},{20,24},{24,28},{1,5},{5,9},{9,... | collective-permute-start | bytes 589832 | tf_op jit(solution)/shard_map/ppermute | solution.py:17
  201.1 541.1 %all-reduce.10.cloned.1.call-start = ((), (), s32[]{:S(2)}) async-start(), calls=%async_computation.1 | async-start | bytes 131072 | tf_op jit(solution)/shard_map/psum | solution.py:96
  (8 other events, 221.9 us)
Sparse Core Ops, SparseCore 0:
  201.2 61.4 all-gather.1
  266.0 476.0 all-reduce.9
where the time goes:
time: 752 us; the launch traced here: 750 us
  waiting for transfers between devices  596 us (79%)
  starting transfers between devices  93.3 us (12%)
  other arithmetic  28.6 us (4%)
  between operations  14.7 us (2%)
  matrix products  11 us (1%)
    psum x1, waiting for transfers between devices, on_device(): gram = lax.psum(gram_part, ('gx', 'gyz')) / total_cells  475 us
    ppermute x16, starting transfers between devices, with_halo(): lax.ppermute(lax.slice_in_dim(block, block.shape[dim] - width, None, axis...  65.6 us
    all_gather x1, waiting for transfers between devices, on_device(): shard_rows = lax.all_gather(filtered, 'band', axis=0, tiled=True)  60.9 us
    ppermute x16, waiting for transfers between devices, with_halo(): lax.ppermute(lax.slice_in_dim(block, block.shape[dim] - width, None, axis...  46.3 us
    ppermute x16, starting transfers between devices, with_halo(): lax.ppermute(lax.slice_in_dim(block, 0, width, axis=dim), axis, backward)  27.6 us
    concatenate x15, other arithmetic, with_halo(): block = jnp.concatenate([low, block, high], axis=dim)  16.2 us
  transfers between devices with their start and end apart: 34, of which 25 were waited for; matrix products, arithmetic and copies ran while one was open for 2% of the time, Pallas kernels for 0%

commit v1 on v0

--- a/solution.py
+++ b/solution.py
@@ -93,7 +93,7 @@
         own_columns, shard_rows, (((0,), (0,)), ((), ())), preferred_element_type=jnp.float32
     )
     gram_part, rotated_flat = (gram_part, rotated_part)
-    gram = lax.psum(gram_part, ("gx", "gyz")) / total_cells
+    gram = jnp.sum(lax.all_gather(gram_part, ("gx", "gyz")), axis=0) / total_cells
     rotated = rotated_flat.reshape(local_slots, size_x, size_y, size_z)
     return (gram, rotated)
 

time: 752 us -> 440 us (0.59)
  waiting for transfers between devices: 596 us -> 279 us
    psum x1 -> x0, waiting for transfers between devices: 475 us -> none  [on_device(): gram = lax.psum(gram_part, ('gx', 'gyz')) / total_cells]
    all_gather x0 -> x1, waiting for transfers between devices: none -> 157 us  [on_device(): lax.all_gather(gram_part, ('gx', 'gyz'))]
  transfers between devices with their start and end apart: 34 -> 34, of which waited for: 25 -> 25; matrix products, arithmetic and copies ran while one was open for 2% -> 3% of each run, Pallas kernels for 0% -> 0%
where the time goes in v1:
time: 440 us; the launch traced here: 435 us
  waiting for transfers between devices  279 us (63%)
  starting transfers between devices  93.3 us (21%)
  other arithmetic  30.2 us (7%)
  between operations  14.7 us (3%)
  matrix products  11 us (2%)
  local copies, waits for them, and re-layouts  7.04 us (2%)
    all_gather x1, waiting for transfers between devices, on_device(): lax.all_gather(gram_part, ('gx', 'gyz'))  157 us
    ppermute x16, starting transfers between devices, with_halo(): lax.ppermute(lax.slice_in_dim(block, block.shape[dim] - width, None, axis...  65.6 us
    all_gather x1, waiting for transfers between devices, on_device(): shard_rows = lax.all_gather(filtered, 'band', axis=0, tiled=True)  61.6 us
    ppermute x16, waiting for transfers between devices, with_halo(): lax.ppermute(lax.slice_in_dim(block, block.shape[dim] - width, None, axis...  46.3 us
    ppermute x16, starting transfers between devices, with_halo(): lax.ppermute(lax.slice_in_dim(block, 0, width, axis=dim), axis, backward)  27.6 us
    concatenate x15, other arithmetic, with_halo(): block = jnp.concatenate([low, block, high], axis=dim)  16.2 us
    ppermute x16, waiting for transfers between devices, with_halo(): lax.ppermute(lax.slice_in_dim(block, 0, width, axis=dim), axis, backward)  13.9 us
    select_n x7, other arithmetic, on_device(): current = jnp.where(active, updated, current)  9.57 us
  transfers between devices with their start and end apart: 34, of which 25 were waited for; matrix products, arithmetic and copies ran while one was open for 3% of the time, Pallas kernels for 0%

profile of v1, /device:TPU:8, one launch (start us, length us, event | category | flops | bytes accessed | tf_op | source)
XLA Modules:
  0.0 435.2 jit_solution(18297733305660152088)
XLA Ops:
  13.8 3.4 multiply_convert_fusion.1
  17.3 3.3 fusion.1
  21.3 3.7 collective-permute-start.2
  25.1 2.1 collective-permute-start.3
  29.3 6.6 %collective-permute-done.3 = f32[64,6,1,128]{3,0,2,1:T(8,128)S(1)} collective-permute-done((f32[64,6,1,128]{3,0,2,1:T(8,128)S(1)}, f32[64,6,1,128]{3,0,2,1:T(8,128)S(1)}, u32[]{:S(2)}, u32[]{:S(2)}) %collective-permute-start.3) | collective-permute-done | bytes 196640 | tf_op jit(solution)/shard_map/ppermute | solution.py:17
  39.2 3.0 collective-permute-start.5
  45.5 3.8 collective-permute-start.7
  51.0 3.5 collective-permute-done.7
  59.2 4.8 %collective-permute-start.9 = (f32[64,1,8,128]{3,0,2,1:T(8,128)S(1)}, f32[64,1,8,128]{3,0,2,1:T(8,128)S(1)}, u32[]{:S(2)}, u32[]{:S(2)}) collective-permute-start(f32[64,1,8,128]{3,0,2,1:T(8,128)S(1)} %get-tuple-element.32), channel_id=1, source_target_pairs={{0,32},{32,64},{64,96},{96,128},{128,160},{160,192},{192,224},{1,3... | collective-permute-start | bytes 786440 | tf_op jit(solution)/shard_map/ppermute | solution.py:17
  67.1 3.9 collective-permute-start.11
  72.7 4.7 %collective-permute-done.11 = f32[64,6,1,128]{3,0,2,1:T(8,128)S(1)} collective-permute-done((f32[64,6,1,128]{3,0,2,1:T(8,128)S(1)}, f32[64,6,1,128]{3,0,2,1:T(8,128)S(1)}, u32[]{:S(2)}, u32[]{:S(2)}) %collective-permute-start.11) | collective-permute-done | bytes 196640 | tf_op jit(solution)/shard_map/ppermute | solution.py:17
  77.4 2.1 select_maximum_fusion.20
  82.6 5.3 %collective-permute-start.13 = (f32[64,1,8,128]{3,0,2,1:T(8,128)S(1)}, f32[64,1,8,128]{3,0,2,1:T(8,128)S(1)}, u32[]{:S(2)}, u32[]{:S(2)}) collective-permute-start(f32[64,1,8,128]{3,0,2,1:T(8,128)S(1)} %get-tuple-element.30), channel_id=1, source_target_pairs={{0,32},{32,64},{64,96},{96,128},{128,160},{160,192},{192,224},{1,3... | collective-permute-start | bytes 786440 | tf_op jit(solution)/shard_map/ppermute | solution.py:17
  91.0 4.1 collective-permute-start.15
  96.6 4.7 %collective-permute-done.15 = f32[64,6,1,128]{3,0,2,1:T(8,128)S(1)} collective-permute-done((f32[64,6,1,128]{3,0,2,1:T(8,128)S(1)}, f32[64,6,1,128]{3,0,2,1:T(8,128)S(1)}, u32[]{:S(2)}, u32[]{:S(2)}) %collective-permute-start.15) | collective-permute-done | bytes 196640 | tf_op jit(solution)/shard_map/ppermute | solution.py:17
  101.3 2.1 select_maximum_fusion.16
  106.7 5.3 %collective-permute-start.17 = (f32[64,1,8,128]{3,0,2,1:T(8,128)S(1)}, f32[64,1,8,128]{3,0,2,1:T(8,128)S(1)}, u32[]{:S(2)}, u32[]{:S(2)}) collective-permute-start(f32[64,1,8,128]{3,0,2,1:T(8,128)S(1)} %get-tuple-element.28), channel_id=1, source_target_pairs={{0,32},{32,64},{64,96},{96,128},{128,160},{160,192},{192,224},{1,3... | collective-permute-start | bytes 786440 | tf_op jit(solution)/shard_map/ppermute | solution.py:17
  115.0 3.9 collective-permute-start.19
  120.7 4.7 %collective-permute-done.19 = f32[64,6,1,128]{3,0,2,1:T(8,128)S(1)} collective-permute-done((f32[64,6,1,128]{3,0,2,1:T(8,128)S(1)}, f32[64,6,1,128]{3,0,2,1:T(8,128)S(1)}, u32[]{:S(2)}, u32[]{:S(2)}) %collective-permute-start.19) | collective-permute-done | bytes 196640 | tf_op jit(solution)/shard_map/ppermute | solution.py:17
  130.1 5.3 %collective-permute-start.21 = (f32[64,1,8,128]{3,0,2,1:T(8,128)S(1)}, f32[64,1,8,128]{3,0,2,1:T(8,128)S(1)}, u32[]{:S(2)}, u32[]{:S(2)}) collective-permute-start(f32[64,1,8,128]{3,0,2,1:T(8,128)S(1)} %get-tuple-element.26), channel_id=1, source_target_pairs={{0,32},{32,64},{64,96},{96,128},{128,160},{160,192},{192,224},{1,3... | collective-permute-start | bytes 786440 | tf_op jit(solution)/shard_map/ppermute | solution.py:17
  138.5 3.9 collective-permute-start.23
  144.2 4.7 %collective-permute-done.23 = f32[64,6,1,128]{3,0,2,1:T(8,128)S(1)} collective-permute-done((f32[64,6,1,128]{3,0,2,1:T(8,128)S(1)}, f32[64,6,1,128]{3,0,2,1:T(8,128)S(1)}, u32[]{:S(2)}, u32[]{:S(2)}) %collective-permute-start.23) | collective-permute-done | bytes 196640 | tf_op jit(solution)/shard_map/ppermute | solution.py:17
  154.0 5.3 %collective-permute-start.25 = (f32[64,1,8,128]{3,0,2,1:T(8,128)S(1)}, f32[64,1,8,128]{3,0,2,1:T(8,128)S(1)}, u32[]{:S(2)}, u32[]{:S(2)}) collective-permute-start(f32[64,1,8,128]{3,0,2,1:T(8,128)S(1)} %get-tuple-element.24), channel_id=1, source_target_pairs={{0,32},{32,64},{64,96},{96,128},{128,160},{160,192},{192,224},{1,3... | collective-permute-start | bytes 786440 | tf_op jit(solution)/shard_map/ppermute | solution.py:17
  162.3 3.9 collective-permute-start.27
  168.0 4.7 %collective-permute-done.27 = f32[64,6,1,128]{3,0,2,1:T(8,128)S(1)} collective-permute-done((f32[64,6,1,128]{3,0,2,1:T(8,128)S(1)}, f32[64,6,1,128]{3,0,2,1:T(8,128)S(1)}, u32[]{:S(2)}, u32[]{:S(2)}) %collective-permute-start.27) | collective-permute-done | bytes 196640 | tf_op jit(solution)/shard_map/ppermute | solution.py:17
  177.4 5.3 %collective-permute-start.29 = (f32[64,1,8,128]{3,0,2,1:T(8,128)S(1)}, f32[64,1,8,128]{3,0,2,1:T(8,128)S(1)}, u32[]{:S(2)}, u32[]{:S(2)}) collective-permute-start(f32[64,1,8,128]{3,0,2,1:T(8,128)S(1)} %get-tuple-element.22), channel_id=1, source_target_pairs={{0,32},{32,64},{64,96},{96,128},{128,160},{160,192},{192,224},{1,3... | collective-permute-start | bytes 786440 | tf_op jit(solution)/shard_map/ppermute | solution.py:17
  185.8 3.9 collective-permute-start.31
  191.4 4.7 %collective-permute-done.31 = f32[64,6,1,128]{3,0,2,1:T(8,128)S(1)} collective-permute-done((f32[64,6,1,128]{3,0,2,1:T(8,128)S(1)}, f32[64,6,1,128]{3,0,2,1:T(8,128)S(1)}, u32[]{:S(2)}, u32[]{:S(2)}) %collective-permute-start.31) | collective-permute-done | bytes 196640 | tf_op jit(solution)/shard_map/ppermute | solution.py:17
  201.1 61.6 %all-gather.4.cloned.1.call-done = bf16[256,4096]{1,0:T(8,128)(2,1)} async-done(((bf16[64,4096]{1,0:T(8,128)(2,1)}), bf16[256,4096]{1,0:T(8,128)(2,1)}) %all-gather.4.cloned.1.call-update) | async-done | bytes 2097168 | tf_op jit(solution)/shard_map/all_gather | solution.py:87
  262.7 3.2 fusion.91
  268.3 157.0 %all-gather.6.cloned.1.call-done = f32[4096,256]{1,0:T(8,128)} async-done(((f32[64,256]{1,0:T(8,128)}), f32[4096,256]{1,0:T(8,128)}) %all-gather.6.cloned.1.call-update) | async-done | bytes 4194320 | tf_op jit(solution)/shard_map/all_gather | solution.py:96
  425.2 2.4 reduce_sum.9
  (102 shorter events, 79.2 us)
Async XLA Ops:
  7.2 255.5 %all-gather.4.cloned.1.call-start = ((), (), s32[]{:S(2)}) async-start(), calls=%async_computation | async-start | bytes 2621440 | tf_op jit(solution)/shard_map/all_gather | solution.py:87
  9.1 11.5 %collective-permute-start.1 = (f32[64,1,8,128]{3,0,2,1:T(8,128)S(1)}, f32[64,1,8,128]{3,0,2,1:T(8,128)S(1)}, u32[]{:S(2)}, u32[]{:S(2)}) collective-permute-start(f32[64,1,8,128]{3,0,2,1:T(8,128)S(1)} %get-tuple-element.37), channel_id=1, source_target_pairs={{0,32},{32,64},{64,96},{96,128},{128,160},{160,192},{192,224},{1,3... | collective-permute-start | bytes 786440 | tf_op jit(solution)/shard_map/ppermute | solution.py:17
  10.9 10.4 %collective-permute-start = (f32[64,1,8,128]{3,0,2,1:T(8,128)S(1)}, f32[64,1,8,128]{3,0,2,1:T(8,128)S(1)}, u32[]{:S(2)}, u32[]{:S(2)}) collective-permute-start(f32[64,1,8,128]{3,0,2,1:T(8,128)S(1)} %get-tuple-element.36), channel_id=1, source_target_pairs={{32,0},{64,32},{96,64},{128,96},{160,128},{192,160},{224,192},{33,... | collective-permute-start | bytes 786440 | tf_op jit(solution)/shard_map/ppermute | solution.py:20
  21.3 8.0 %collective-permute-start.2 = (f32[64,6,1,128]{3,0,2,1:T(8,128)S(1)}, f32[64,6,1,128]{3,0,2,1:T(8,128)S(1)}, u32[]{:S(2)}, u32[]{:S(2)}) collective-permute-start(f32[64,6,1,128]{3,0,2,1:T(8,128)S(1)} %get-tuple-element.21), channel_id=1, source_target_pairs={{4,0},{8,4},{12,8},{16,12},{20,16},{24,20},{28,24},{5,1},{9,5},{13... | collective-permute-start | bytes 589832 | tf_op jit(solution)/shard_map/ppermute | solution.py:20
  25.1 10.9 %collective-permute-start.3 = (f32[64,6,1,128]{3,0,2,1:T(8,128)S(1)}, f32[64,6,1,128]{3,0,2,1:T(8,128)S(1)}, u32[]{:S(2)}, u32[]{:S(2)}) collective-permute-start(f32[64,6,1,128]{3,0,2,1:T(8,128)S(1)} %get-tuple-element.20), channel_id=1, source_target_pairs={{0,4},{4,8},{8,12},{12,16},{16,20},{20,24},{24,28},{1,5},{5,9},{9,... | collective-permute-start | bytes 589832 | tf_op jit(solution)/shard_map/ppermute | solution.py:17
  43.4 7.6 %collective-permute-start.6 = (f32[64,6,1,128]{3,0,2,1:T(8,128)S(1)}, f32[64,6,1,128]{3,0,2,1:T(8,128)S(1)}, u32[]{:S(2)}, u32[]{:S(2)}) collective-permute-start(f32[64,6,1,128]{3,0,2,1:T(8,128)S(1)} %get-tuple-element.19), channel_id=1, source_target_pairs={{4,0},{8,4},{12,8},{16,12},{20,16},{24,20},{28,24},{5,1},{9,5},{13... | collective-permute-start | bytes 589832 | tf_op jit(solution)/shard_map/ppermute | solution.py:20
  45.5 9.0 %collective-permute-start.7 = (f32[64,6,1,128]{3,0,2,1:T(8,128)S(1)}, f32[64,6,1,128]{3,0,2,1:T(8,128)S(1)}, u32[]{:S(2)}, u32[]{:S(2)}) collective-permute-start(f32[64,6,1,128]{3,0,2,1:T(8,128)S(1)} %get-tuple-element.18), channel_id=1, source_target_pairs={{0,4},{4,8},{8,12},{12,16},{16,20},{20,24},{24,28},{1,5},{5,9},{9,... | collective-permute-start | bytes 589832 | tf_op jit(solution)/shard_map/ppermute | solution.py:17
  57.9 6.1 %collective-permute-start.8 = (f32[64,1,8,128]{3,0,2,1:T(8,128)S(1)}, f32[64,1,8,128]{3,0,2,1:T(8,128)S(1)}, u32[]{:S(2)}, u32[]{:S(2)}) collective-permute-start(f32[64,1,8,128]{3,0,2,1:T(8,128)S(1)} %get-tuple-element.33), channel_id=1, source_target_pairs={{32,0},{64,32},{96,64},{128,96},{160,128},{192,160},{224,192},{33,... | collective-permute-start | bytes 786440 | tf_op jit(solution)/shard_map/ppermute | solution.py:20
  59.2 5.9 %collective-permute-start.9 = (f32[64,1,8,128]{3,0,2,1:T(8,128)S(1)}, f32[64,1,8,128]{3,0,2,1:T(8,128)S(1)}, u32[]{:S(2)}, u32[]{:S(2)}) collective-permute-start(f32[64,1,8,128]{3,0,2,1:T(8,128)S(1)} %get-tuple-element.32), channel_id=1, source_target_pairs={{0,32},{32,64},{64,96},{96,128},{128,160},{160,192},{192,224},{1,3... | collective-permute-start | bytes 786440 | tf_op jit(solution)/shard_map/ppermute | solution.py:17
  65.1 7.6 %collective-permute-start.10 = (f32[64,6,1,128]{3,0,2,1:T(8,128)S(1)}, f32[64,6,1,128]{3,0,2,1:T(8,128)S(1)}, u32[]{:S(2)}, u32[]{:S(2)}) collective-permute-start(f32[64,6,1,128]{3,0,2,1:T(8,128)S(1)} %get-tuple-element.17), channel_id=1, source_target_pairs={{4,0},{8,4},{12,8},{16,12},{20,16},{24,20},{28,24},{5,1},{9,5},{13... | collective-permute-start | bytes 589832 | tf_op jit(solution)/shard_map/ppermute | solution.py:20
  67.1 10.4 %collective-permute-start.11 = (f32[64,6,1,128]{3,0,2,1:T(8,128)S(1)}, f32[64,6,1,128]{3,0,2,1:T(8,128)S(1)}, u32[]{:S(2)}, u32[]{:S(2)}) collective-permute-start(f32[64,6,1,128]{3,0,2,1:T(8,128)S(1)} %get-tuple-element.16), channel_id=1, source_target_pairs={{0,4},{4,8},{8,12},{12,16},{16,20},{20,24},{24,28},{1,5},{5,9},{9,... | collective-permute-start | bytes 589832 | tf_op jit(solution)/shard_map/ppermute | solution.py:17
  81.3 6.6 %collective-permute-start.12 = (f32[64,1,8,128]{3,0,2,1:T(8,128)S(1)}, f32[64,1,8,128]{3,0,2,1:T(8,128)S(1)}, u32[]{:S(2)}, u32[]{:S(2)}) collective-permute-start(f32[64,1,8,128]{3,0,2,1:T(8,128)S(1)} %get-tuple-element.31), channel_id=1, source_target_pairs={{32,0},{64,32},{96,64},{128,96},{160,128},{192,160},{224,192},{33,... | collective-permute-start | bytes 786440 | tf_op jit(solution)/shard_map/ppermute | solution.py:20
  82.6 6.4 %collective-permute-start.13 = (f32[64,1,8,128]{3,0,2,1:T(8,128)S(1)}, f32[64,1,8,128]{3,0,2,1:T(8,128)S(1)}, u32[]{:S(2)}, u32[]{:S(2)}) collective-permute-start(f32[64,1,8,128]{3,0,2,1:T(8,128)S(1)} %get-tuple-element.30), channel_id=1, source_target_pairs={{0,32},{32,64},{64,96},{96,128},{128,160},{160,192},{192,224},{1,3... | collective-permute-start | bytes 786440 | tf_op jit(solution)/shard_map/ppermute | solution.py:17
  89.0 7.6 %collective-permute-start.14 = (f32[64,6,1,128]{3,0,2,1:T(8,128)S(1)}, f32[64,6,1,128]{3,0,2,1:T(8,128)S(1)}, u32[]{:S(2)}, u32[]{:S(2)}) collective-permute-start(f32[64,6,1,128]{3,0,2,1:T(8,128)S(1)} %get-tuple-element.15), channel_id=1, source_target_pairs={{4,0},{8,4},{12,8},{16,12},{20,16},{24,20},{28,24},{5,1},{9,5},{13... | collective-permute-start | bytes 589832 | tf_op jit(solution)/shard_map/ppermute | solution.py:20
  91.0 10.4 %collective-permute-start.15 = (f32[64,6,1,128]{3,0,2,1:T(8,128)S(1)}, f32[64,6,1,128]{3,0,2,1:T(8,128)S(1)}, u32[]{:S(2)}, u32[]{:S(2)}) collective-permute-start(f32[64,6,1,128]{3,0,2,1:T(8,128)S(1)} %get-tuple-element.14), channel_id=1, source_target_pairs={{0,4},{4,8},{8,12},{12,16},{16,20},{20,24},{24,28},{1,5},{5,9},{9,... | collective-permute-start | bytes 589832 | tf_op jit(solution)/shard_map/ppermute | solution.py:17
  105.4 6.6 %collective-permute-start.16 = (f32[64,1,8,128]{3,0,2,1:T(8,128)S(1)}, f32[64,1,8,128]{3,0,2,1:T(8,128)S(1)}, u32[]{:S(2)}, u32[]{:S(2)}) collective-permute-start(f32[64,1,8,128]{3,0,2,1:T(8,128)S(1)} %get-tuple-element.29), channel_id=1, source_target_pairs={{32,0},{64,32},{96,64},{128,96},{160,128},{192,160},{224,192},{33,... | collective-permute-start | bytes 786440 | tf_op jit(solution)/shard_map/ppermute | solution.py:20
  106.7 6.4 %collective-permute-start.17 = (f32[64,1,8,128]{3,0,2,1:T(8,128)S(1)}, f32[64,1,8,128]{3,0,2,1:T(8,128)S(1)}, u32[]{:S(2)}, u32[]{:S(2)}) collective-permute-start(f32[64,1,8,128]{3,0,2,1:T(8,128)S(1)} %get-tuple-element.28), channel_id=1, source_target_pairs={{0,32},{32,64},{64,96},{96,128},{128,160},{160,192},{192,224},{1,3... | collective-permute-start | bytes 786440 | tf_op jit(solution)/shard_map/ppermute | solution.py:17
  113.1 7.6 %collective-permute-start.18 = (f32[64,6,1,128]{3,0,2,1:T(8,128)S(1)}, f32[64,6,1,128]{3,0,2,1:T(8,128)S(1)}, u32[]{:S(2)}, u32[]{:S(2)}) collective-permute-start(f32[64,6,1,128]{3,0,2,1:T(8,128)S(1)} %get-tuple-element.13), channel_id=1, source_target_pairs={{4,0},{8,4},{12,8},{16,12},{20,16},{24,20},{28,24},{5,1},{9,5},{13... | collective-permute-start | bytes 589832 | tf_op jit(solution)/shard_map/ppermute | solution.py:20
  115.0 10.4 %collective-permute-start.19 = (f32[64,6,1,128]{3,0,2,1:T(8,128)S(1)}, f32[64,6,1,128]{3,0,2,1:T(8,128)S(1)}, u32[]{:S(2)}, u32[]{:S(2)}) collective-permute-start(f32[64,6,1,128]{3,0,2,1:T(8,128)S(1)} %get-tuple-element.12), channel_id=1, source_target_pairs={{0,4},{4,8},{8,12},{12,16},{16,20},{20,24},{24,28},{1,5},{5,9},{9,... | collective-permute-start | bytes 589832 | tf_op jit(solution)/shard_map/ppermute | solution.py:17
  128.8 6.6 %collective-permute-start.20 = (f32[64,1,8,128]{3,0,2,1:T(8,128)S(1)}, f32[64,1,8,128]{3,0,2,1:T(8,128)S(1)}, u32[]{:S(2)}, u32[]{:S(2)}) collective-permute-start(f32[64,1,8,128]{3,0,2,1:T(8,128)S(1)} %get-tuple-element.27), channel_id=1, source_target_pairs={{32,0},{64,32},{96,64},{128,96},{160,128},{192,160},{224,192},{33,... | collective-permute-start | bytes 786440 | tf_op jit(solution)/shard_map/ppermute | solution.py:20
  130.1 6.4 %collective-permute-start.21 = (f32[64,1,8,128]{3,0,2,1:T(8,128)S(1)}, f32[64,1,8,128]{3,0,2,1:T(8,128)S(1)}, u32[]{:S(2)}, u32[]{:S(2)}) collective-permute-start(f32[64,1,8,128]{3,0,2,1:T(8,128)S(1)} %get-tuple-element.26), channel_id=1, source_target_pairs={{0,32},{32,64},{64,96},{96,128},{128,160},{160,192},{192,224},{1,3... | collective-permute-start | bytes 786440 | tf_op jit(solution)/shard_map/ppermute | solution.py:17
  136.6 7.6 %collective-permute-start.22 = (f32[64,6,1,128]{3,0,2,1:T(8,128)S(1)}, f32[64,6,1,128]{3,0,2,1:T(8,128)S(1)}, u32[]{:S(2)}, u32[]{:S(2)}) collective-permute-start(f32[64,6,1,128]{3,0,2,1:T(8,128)S(1)} %get-tuple-element.11), channel_id=1, source_target_pairs={{4,0},{8,4},{12,8},{16,12},{20,16},{24,20},{28,24},{5,1},{9,5},{13... | collective-permute-start | bytes 589832 | tf_op jit(solution)/shard_map/ppermute | solution.py:20
  138.5 10.4 %collective-permute-start.23 = (f32[64,6,1,128]{3,0,2,1:T(8,128)S(1)}, f32[64,6,1,128]{3,0,2,1:T(8,128)S(1)}, u32[]{:S(2)}, u32[]{:S(2)}) collective-permute-start(f32[64,6,1,128]{3,0,2,1:T(8,128)S(1)} %get-tuple-element.10), channel_id=1, source_target_pairs={{0,4},{4,8},{8,12},{12,16},{16,20},{20,24},{24,28},{1,5},{5,9},{9,... | collective-permute-start | bytes 589832 | tf_op jit(solution)/shard_map/ppermute | solution.py:17
  152.7 6.6 %collective-permute-start.24 = (f32[64,1,8,128]{3,0,2,1:T(8,128)S(1)}, f32[64,1,8,128]{3,0,2,1:T(8,128)S(1)}, u32[]{:S(2)}, u32[]{:S(2)}) collective-permute-start(f32[64,1,8,128]{3,0,2,1:T(8,128)S(1)} %get-tuple-element.25), channel_id=1, source_target_pairs={{32,0},{64,32},{96,64},{128,96},{160,128},{192,160},{224,192},{33,... | collective-permute-start | bytes 786440 | tf_op jit(solution)/shard_map/ppermute | solution.py:20
  154.0 6.4 %collective-permute-start.25 = (f32[64,1,8,128]{3,0,2,1:T(8,128)S(1)}, f32[64,1,8,128]{3,0,2,1:T(8,128)S(1)}, u32[]{:S(2)}, u32[]{:S(2)}) collective-permute-start(f32[64,1,8,128]{3,0,2,1:T(8,128)S(1)} %get-tuple-element.24), channel_id=1, source_target_pairs={{0,32},{32,64},{64,96},{96,128},{128,160},{160,192},{192,224},{1,3... | collective-permute-start | bytes 786440 | tf_op jit(solution)/shard_map/ppermute | solution.py:17
  160.4 7.6 %collective-permute-start.26 = (f32[64,6,1,128]{3,0,2,1:T(8,128)S(1)}, f32[64,6,1,128]{3,0,2,1:T(8,128)S(1)}, u32[]{:S(2)}, u32[]{:S(2)}) collective-permute-start(f32[64,6,1,128]{3,0,2,1:T(8,128)S(1)} %get-tuple-element.9), channel_id=1, source_target_pairs={{4,0},{8,4},{12,8},{16,12},{20,16},{24,20},{28,24},{5,1},{9,5},{13... | collective-permute-start | bytes 589832 | tf_op jit(solution)/shard_map/ppermute | solution.py:20
  162.3 10.4 %collective-permute-start.27 = (f32[64,6,1,128]{3,0,2,1:T(8,128)S(1)}, f32[64,6,1,128]{3,0,2,1:T(8,128)S(1)}, u32[]{:S(2)}, u32[]{:S(2)}) collective-permute-start(f32[64,6,1,128]{3,0,2,1:T(8,128)S(1)} %get-tuple-element.8), channel_id=1, source_target_pairs={{0,4},{4,8},{8,12},{12,16},{16,20},{20,24},{24,28},{1,5},{5,9},{9,... | collective-permute-start | bytes 589832 | tf_op jit(solution)/shard_map/ppermute | solution.py:17
  176.1 6.6 %collective-permute-start.28 = (f32[64,1,8,128]{3,0,2,1:T(8,128)S(1)}, f32[64,1,8,128]{3,0,2,1:T(8,128)S(1)}, u32[]{:S(2)}, u32[]{:S(2)}) collective-permute-start(f32[64,1,8,128]{3,0,2,1:T(8,128)S(1)} %get-tuple-element.23), channel_id=1, source_target_pairs={{32,0},{64,32},{96,64},{128,96},{160,128},{192,160},{224,192},{33,... | collective-permute-start | bytes 786440 | tf_op jit(solution)/shard_map/ppermute | solution.py:20
  177.4 6.4 %collective-permute-start.29 = (f32[64,1,8,128]{3,0,2,1:T(8,128)S(1)}, f32[64,1,8,128]{3,0,2,1:T(8,128)S(1)}, u32[]{:S(2)}, u32[]{:S(2)}) collective-permute-start(f32[64,1,8,128]{3,0,2,1:T(8,128)S(1)} %get-tuple-element.22), channel_id=1, source_target_pairs={{0,32},{32,64},{64,96},{96,128},{128,160},{160,192},{192,224},{1,3... | collective-permute-start | bytes 786440 | tf_op jit(solution)/shard_map/ppermute | solution.py:17
  183.9 7.6 %collective-permute-start.30 = (f32[64,6,1,128]{3,0,2,1:T(8,128)S(1)}, f32[64,6,1,128]{3,0,2,1:T(8,128)S(1)}, u32[]{:S(2)}, u32[]{:S(2)}) collective-permute-start(f32[64,6,1,128]{3,0,2,1:T(8,128)S(1)} %get-tuple-element.7), channel_id=1, source_target_pairs={{4,0},{8,4},{12,8},{16,12},{20,16},{24,20},{28,24},{5,1},{9,5},{13... | collective-permute-start | bytes 589832 | tf_op jit(solution)/shard_map/ppermute | solution.py:20
  185.8 10.4 %collective-permute-start.31 = (f32[64,6,1,128]{3,0,2,1:T(8,128)S(1)}, f32[64,6,1,128]{3,0,2,1:T(8,128)S(1)}, u32[]{:S(2)}, u32[]{:S(2)}) collective-permute-start(f32[64,6,1,128]{3,0,2,1:T(8,128)S(1)} %get-tuple-element.6), channel_id=1, source_target_pairs={{0,4},{4,8},{8,12},{12,16},{16,20},{20,24},{24,28},{1,5},{5,9},{9,... | collective-permute-start | bytes 589832 | tf_op jit(solution)/shard_map/ppermute | solution.py:17
  201.1 224.2 %all-gather.6.cloned.1.call-start = ((), (), s32[]{:S(2)}) async-start(), calls=%async_computation.1 | async-start | bytes 4259840 | tf_op jit(solution)/shard_map/all_gather | solution.py:96
  (8 other events, 350.7 us)
Sparse Core Ops, SparseCore 0:
  201.2 61.4 all-gather.3
  266.0 159.1 all-gather.5
